TPU v7x, 128 devices: a whole 4x4x4 slice. The times are simulated.
128 devices in a mesh: ctx: 16 (over x, y), head: 8 (over z, core).
Axes of the slice: x: 4, y: 4, z: 4, core: 2. Of those that a mesh axis runs over, the one named last changes fastest.
Arguments:
- lin_query: bfloat16 [8192, 8192], P('ctx', 'head'), may hold values from -6 to 6
- lin_key: bfloat16 [8192, 8192], P('ctx', 'head'), may hold values from -6 to 6
- lin_value: bfloat16 [8192, 8192], P('ctx', 'head'), may hold values from -61.2 to 61.2
- lin_gate: bfloat16 [8192, 8192], P('ctx', 'head'), may hold values from -6 to 6
- norm_gain: float32 [8192], P('head'), may hold values from 0.25 to 1.75
- soft_query: bfloat16 [8192, 8192], P('ctx', 'head'), may hold values from -4.5 to 4.5
- soft_key: bfloat16 [8192, 1024], P('ctx', 'head'), may hold values from -4.5 to 4.5
- soft_value: bfloat16 [8192, 1024], P('ctx', 'head'), may hold values from -6 to 6
- doc_lengths: int32 [8], replicated, may hold values from 1 to 4096, 8192 in all
Outputs:
- lin_out: bfloat16 [8192, 8192], P('ctx', 'head')
- soft_out: bfloat16 [8192, 8192], P('ctx', 'head')
Inputs may be any that keep to these rules, and one draw needn't show every extreme that they name: `doc_lengths`: the lengths sum to 8192.
All inputs are finite; a program needn't handle non-finite values.
Results may differ from a plain program's by a relative error of at most 0.012.
Values may be sent and summed in bfloat16 or wider, within the bound.
No kernel may reach another device: no remote copies, remote signals or barrier semaphores. Data moves between devices by JAX's collectives and lax.ppermute only.
A program may use at most 128 MiB of HBM per device.

v0:
```python
import functools

import jax
import jax.numpy as jnp
from jax import lax
from jax.experimental import pallas as pl
from jax.experimental.pallas import tpu as pltpu
from jax.sharding import PartitionSpec as P

HEADS = 64
HEAD_DIM = 128
DOCS = 8
EPS = 1e-06
ROWS = 512
LOCAL = 8
WINDOW = 8
FAR = -1.0e4
SCALE = HEAD_DIM**-0.5 * 1.4426950408889634
f32, bf16, i32 = jnp.float32, jnp.bfloat16, jnp.int32

SMEM = pl.BlockSpec(memory_space=pltpu.SMEM)
VMEM = pl.BlockSpec(memory_space=pltpu.VMEM)
ANY = pl.BlockSpec(memory_space=pl.ANY)
LIGHT = pl.CostEstimate(flops=10**6, bytes_accessed=2**16, transcendentals=0)
SMALL = pltpu.CompilerParams(vmem_limit_bytes=16 * 2**20)


def doc_starts(lens):
    starts = [jnp.int32(0)]
    for d in range(DOCS - 1):
        starts.append(starts[-1] + lens[d])
    return starts


def start_of(starts, pos):
    at = starts[0]
    for s in starts[1:]:
        at = jnp.where(pos >= s, s, at)
    return at


def end_of(starts, pos):
    at = jnp.int32(2**30)
    for s in reversed(starts[1:]):
        at = jnp.where(pos < s, s, at)
    return at


def first_row():
    return lax.axis_index("ctx") * ROWS


def dot_nt(a, b):
    return lax.dot_general(a, b, (((1,), (1,)), ((), ())), preferred_element_type=f32)


def dot_tn(a, b):
    return lax.dot_general(a, b, (((0,), (0,)), ((), ())), preferred_element_type=f32)


def head_cols(h):
    return slice(h * HEAD_DIM, (h + 1) * HEAD_DIM)


def linear_kernel(place, lens, q_ref, k_ref, v_ref, raw_ref, state_ref, mask):
    row0 = place[0] * ROWS
    starts = doc_starts(lens)

    @pl.when(pl.program_id(0) == 0)
    def _():
        rows = lax.broadcasted_iota(i32, (ROWS, ROWS), 0)
        cols = lax.broadcasted_iota(i32, (ROWS, ROWS), 1)
        pos = row0 + lax.broadcasted_iota(i32, (ROWS, 1), 0)
        begin = start_of(starts, pos) - row0
        mask[...] = jnp.where((cols <= rows) & (cols >= begin), 1.0, 0.0).astype(bf16)

    last_begin = start_of(starts, row0 + ROWS - 1) - row0
    keep = lax.broadcasted_iota(i32, (HEAD_DIM, ROWS), 1) >= last_begin
    keep = jnp.where(keep, 1.0, 0.0).astype(bf16)
    half = ROWS // 2
    for h in range(q_ref.shape[1] // HEAD_DIM):
        c = head_cols(h)
        state_ref[c, :] = jnp.dot(
            k_ref[:, c].T * keep, v_ref[:, c], preferred_element_type=f32
        ).astype(bf16)
        for r, width in ((0, half), (half, ROWS)):
            rows = slice(r, r + half)
            s = dot_nt(q_ref[rows, c], k_ref[:width, c]).astype(bf16) * mask[rows, :width]
            raw_ref[rows, c] = jnp.dot(s, v_ref[:width, c], preferred_element_type=f32)


def linear_call(place, lens, q, k, v):
    step = 4 * HEAD_DIM
    block = pl.BlockSpec((ROWS, step), lambda g: (0, g))
    return pl.pallas_call(
        linear_kernel,
        grid=(LOCAL * HEAD_DIM // step,),
        in_specs=[SMEM, SMEM, block, block, block],
        out_specs=(block, pl.BlockSpec((step, HEAD_DIM), lambda g: (g, 0))),
        out_shape=(
            jax.ShapeDtypeStruct((ROWS, LOCAL * HEAD_DIM), f32),
            jax.ShapeDtypeStruct((LOCAL * HEAD_DIM, HEAD_DIM), bf16),
        ),
        scratch_shapes=[pltpu.VMEM((ROWS, ROWS), bf16)],
        cost_estimate=LIGHT,
        name="linear",
    )(place, lens, q, k, v)


def join_kernel(distance, place, lens, own_ref, got_ref, out_ref):
    row0 = place[0] * ROWS
    same = start_of(doc_starts(lens), row0 + ROWS - 1) < row0 - (distance - 1) * ROWS
    take = jnp.where(same & (place[0] >= distance), 1.0, 0.0)
    out_ref[...] = (own_ref[...].astype(f32) + take * got_ref[...].astype(f32)).astype(bf16)


def join_call(distance, place, lens, own, got):
    return pl.pallas_call(
        functools.partial(join_kernel, distance),
        in_specs=[SMEM, SMEM, VMEM, VMEM],
        out_specs=VMEM,
        out_shape=jax.ShapeDtypeStruct(own.shape, bf16),
        compiler_params=SMALL,
        cost_estimate=LIGHT,
        name=f"join{distance}",
    )(place, lens, own, got)


def inter_kernel(place, lens, q_ref, near_ref, far_ref, raw_ref, out_ref, square_ref):
    row0 = place[0] * ROWS
    starts = doc_starts(lens)
    reach = jnp.where(place[0] > 0, end_of(starts, row0 - 1) - row0, 0)
    inside = lax.broadcasted_iota(i32, (ROWS, HEAD_DIM), 0) < reach
    take = jnp.where(
        (start_of(starts, row0 - 1) < row0 - 2 * ROWS) & (place[0] >= 3), 1.0, 0.0
    )
    squares = jnp.zeros((ROWS, HEAD_DIM), f32)
    for h in range(LOCAL):
        c = head_cols(h)
        state = (near_ref[c, :].astype(f32) + take * far_ref[c, :].astype(f32)).astype(bf16)
        carried = jnp.dot(q_ref[:, c], state, preferred_element_type=f32)
        raw = raw_ref[:, c] + jnp.where(inside, carried, 0.0)
        out_ref[:, c] = raw
        squares = squares + raw * raw
    ones = jnp.ones((8, HEAD_DIM), f32)
    square_ref[...] = lax.dot_general(
        ones, squares, (((1,), (1,)), ((), ())), precision=lax.Precision.HIGHEST,
        preferred_element_type=f32,
    )


def inter_call(place, lens, q, near, far, raw):
    return pl.pallas_call(
        inter_kernel,
        in_specs=[SMEM, SMEM] + [VMEM] * 4,
        out_specs=(VMEM, VMEM),
        out_shape=(
            jax.ShapeDtypeStruct(raw.shape, f32),
            jax.ShapeDtypeStruct((8, ROWS), f32),
        ),
        input_output_aliases={5: 0},
        compiler_params=SMALL,
        cost_estimate=LIGHT,
        name="inter",
    )(place, lens, q, near, far, raw)


def norm_kernel(raw_ref, gate_ref, gain_ref, near_ref, far_ref, out_ref, inverse):
    @pl.when(pl.program_id(0) == 0)
    def _():
        ones = jnp.full((8, HEAD_DIM), 0.125, f32)
        total = lax.dot_general(
            near_ref[...] + far_ref[...], ones, (((0,), (0,)), ((), ())),
            precision=lax.Precision.HIGHEST, preferred_element_type=f32,
        )
        inverse[...] = lax.rsqrt(total / (HEADS * HEAD_DIM) + EPS)

    for h in range(raw_ref.shape[1] // HEAD_DIM):
        c = head_cols(h)
        gate = jax.nn.sigmoid(gate_ref[:, c].astype(f32))
        out_ref[:, c] = (raw_ref[:, c] * inverse[...] * gain_ref[:, c] * gate).astype(bf16)


def norm_call(raw, gate, gain, near, far):
    step = 4 * HEAD_DIM
    block = pl.BlockSpec((ROWS, step), lambda g: (0, g))
    square = pl.BlockSpec((8, ROWS), lambda g: (0, 0))
    return pl.pallas_call(
        norm_kernel,
        grid=(LOCAL * HEAD_DIM // step,),
        in_specs=[block, block, pl.BlockSpec((1, step), lambda g: (0, g)), square, square],
        out_specs=block,
        out_shape=jax.ShapeDtypeStruct((ROWS, LOCAL * HEAD_DIM), bf16),
        scratch_shapes=[pltpu.VMEM((ROWS, HEAD_DIM), f32)],
        compiler_params=SMALL,
        cost_estimate=LIGHT,
        name="norm",
    )(raw, gate, gain, near, far)


def attend_kernel(offsets, own, first, last, *refs):
    refs = list(refs)
    place, lens, q_ref = refs[:3]
    del refs[:3]
    count = len(offsets)
    every = tuple(range(WINDOW + 1)) if last else ()
    own_ref = refs.pop(0) if own else None
    shard_refs = [refs.pop(0) for _ in offsets]
    every_refs = [refs.pop(0) for _ in every]
    if not first:
        acc, part = refs.pop(0), refs.pop(0)
    if last:
        out_ref = refs.pop(0)
    else:
        acc, part = refs.pop(0), refs.pop(0)
    if first:
        queries = refs.pop(0)
    else:
        queries = q_ref
    bias, held, sems = refs

    row0 = place[0] * ROWS
    starts = doc_starts(lens)
    first_start, last_start = start_of(starts, row0), start_of(starts, row0 + ROWS - 1)

    def needed(offset):
        begin = row0 - offset * ROWS
        return (begin >= 0) & (first_start < begin + ROWS)

    def copy(ref, slot):
        return pltpu.make_async_copy(ref, held.at[slot], sems.at[slot])

    for slot, offset in enumerate(offsets):

        @pl.when(needed(offset))
        def _(slot=slot):
            copy(shard_refs[slot], slot).start()

    if first:
        queries[...] = (q_ref[...].astype(f32) * SCALE).astype(bf16)
        part[...] = jnp.zeros_like(part)
        acc[...] = jnp.zeros_like(acc)

    def set_bias(offset, causal):
        pos = row0 + lax.broadcasted_iota(i32, (ROWS, 1), 0)
        begin = start_of(starts, pos)
        keys = row0 - offset * ROWS + lax.broadcasted_iota(i32, (ROWS, ROWS), 1)
        allowed = keys >= begin
        if causal:
            allowed = allowed & (keys <= row0 + lax.broadcasted_iota(i32, (ROWS, ROWS), 0))
        bias[...] = jnp.where(allowed, 0.0, FAR)

    def add(rows, c, keys, values, width, masked):
        s = dot_nt(queries[rows, c], keys)
        if masked:
            s = s + bias[rows, :width]
        p = jnp.exp2(s)
        acc[rows, c] += jnp.dot(p.astype(bf16), values, preferred_element_type=f32)
        sums = p[:, :HEAD_DIM]
        for at in range(HEAD_DIM, width, HEAD_DIM):
            sums = sums + p[:, at : at + HEAD_DIM]
        part[rows, c] += sums

    if own:
        set_bias(0, True)
        half = ROWS // 2
        for h in range(LOCAL):
            for r, width in ((0, half), (half, ROWS)):
                rows = slice(r, r + half)
                add(rows, head_cols(h), own_ref[:width, :], own_ref[ROWS : ROWS + width, :], width, True)

    def one(slot, _):
        offset = jnp.int32(offsets[0])
        for i in range(1, count):
            offset = jnp.where(slot == i, offsets[i], offset)
        use = needed(offset)
        free = last_start <= row0 - offset * ROWS

        def every_head(masked):
            for h in range(LOCAL):
                add(slice(None), head_cols(h), held[slot, :ROWS, :], held[slot, ROWS:, :], ROWS, masked)

        @pl.when(use)
        def _():
            copy(shard_refs[0], slot).wait()

        @pl.when(use)
        def _():
            @pl.when(free)
            def _():
                bias[...] = jnp.zeros_like(bias)

            @pl.when(jnp.logical_not(free))
            def _():
                set_bias(offset, False)

            every_head(True)

        return 0

    if count:
        lax.fori_loop(0, count, one, 0)
    if not last:
        return

    low = high = jnp.ones((ROWS, 1), f32)
    for h in range(LOCAL):
        c = head_cols(h)
        total = jnp.sum(part[:, c], axis=1, keepdims=True)
        low, high = jnp.minimum(low, total), jnp.maximum(high, total)
        out_ref[:, c] = (acc[:, c] / total).astype(bf16)

    @pl.when((jnp.min(low) < 2.0**-60) | (jnp.max(high) > 2.0**100))
    def _():
        lane = lax.broadcasted_iota(i32, (ROWS, HEAD_DIM), 1)
        acc[...] = jnp.zeros_like(acc)
        for h in range(LOCAL):
            part[:, head_cols(h)] = jnp.where(lane == 0, -1.0e30, 0.0)
        def again(offset, _):
            for k in every:

                @pl.when(offset == k)
                def _(k=k):
                    fetch = pltpu.make_async_copy(every_refs[k], held.at[0], sems.at[0])
                    fetch.start()
                    fetch.wait()

            set_bias(offset, True)

            def one_head(h, _):
                c = pl.ds(pl.multiple_of(h * HEAD_DIM, HEAD_DIM), HEAD_DIM)
                s = dot_nt(queries[:, c], held[0, :ROWS, :]) + bias[...]
                old = part[:, c]
                peak, gone = old[:, 0:1], old[:, 1:2]
                new = jnp.maximum(peak, jnp.max(s, axis=1, keepdims=True))
                p = jnp.exp2(s - new)
                shrink = jnp.exp2(peak - new)
                acc[:, c] = acc[:, c] * shrink + jnp.dot(
                    p.astype(bf16), held[0, ROWS:, :], preferred_element_type=f32
                )
                gone = gone * shrink + jnp.sum(p, axis=1, keepdims=True)
                part[:, c] = jnp.where(lane == 0, new, gone)
                return 0

            lax.fori_loop(0, LOCAL, one_head, 0)
            return 0

        lax.fori_loop(0, jnp.minimum(place[0], WINDOW) + 1, again, 0)
        for h in range(LOCAL):
            c = head_cols(h)
            out_ref[:, c] = (acc[:, c] / part[:, c][:, 1:2]).astype(bf16)


def attend_call(place, lens, q, shards, sums, own, offsets, last, name):
    first = sums is None
    wide = q.shape
    operands, specs = [place, lens, q if first else sums[2]], [SMEM, SMEM, VMEM]
    if own:
        operands.append(shards[0])
        specs.append(VMEM)
    operands += [shards[o] for o in offsets]
    specs += [ANY] * len(offsets)
    if last:
        operands += [shards[o] for o in range(WINDOW + 1)]
        specs += [ANY] * (WINDOW + 1)
    if not first:
        operands += list(sums[:2])
        specs += [VMEM, VMEM]
    scratch = [
        pltpu.VMEM((ROWS, ROWS), f32),
        pltpu.VMEM((max(1, len(offsets)), 2 * ROWS, HEAD_DIM), bf16),
        pltpu.SemaphoreType.DMA((max(1, len(offsets)),)),
    ]
    aliases = {}
    if last:
        out_shape = jax.ShapeDtypeStruct(wide, bf16)
        out_specs = VMEM
    else:
        out_shape = [jax.ShapeDtypeStruct(wide, f32)] * 2
        if first:
            out_shape.append(jax.ShapeDtypeStruct(wide, bf16))
        else:
            aliases = {len(operands) - 2: 0, len(operands) - 1: 1}
        out_specs = [VMEM] * len(out_shape)
    result = pl.pallas_call(
        functools.partial(attend_kernel, tuple(offsets), own, first, last),
        input_output_aliases=aliases,
        in_specs=specs,
        out_specs=out_specs,
        out_shape=out_shape,
        scratch_shapes=scratch,
        compiler_params=pltpu.CompilerParams(vmem_limit_bytes=20 * 2**20),
        cost_estimate=LIGHT,
        name=name,
    )(*operands)
    if last or first:
        return result
    return [*result, sums[2]]


def rotate(a, distance):
    return lax.ppermute(a, "ctx", [(c, (c + distance) % 16) for c in range(16)])


def turn(a, distance):
    return lax.ppermute(
        a, "ctx", [(4 * x + y, 4 * x + (y + distance) % 4) for x in range(4) for y in range(4)]
    )


def head_swap(a, bit):
    return lax.ppermute(a, "head", [(i, i ^ bit) for i in range(8)])


def after(a, *others):
    return lax.optimization_barrier((a, *others))[0]


def body(
    lin_query, lin_key, lin_value, lin_gate, norm_gain, soft_query, soft_key, soft_value, doc_lengths
):
    place = jnp.reshape(lax.axis_index("ctx"), (1,))
    y = lax.axis_index("ctx") % 4
    gain = norm_gain.reshape(1, -1)

    def behind(distance, here, there):
        return turn(jnp.where(y >= 4 - distance, there, here), distance)

    def attend(place, sums, own, offsets, last, name):
        return attend_call(place, doc_lengths, soft_query, shards, sums, own, offsets, last, name)

    own = jnp.concatenate([soft_key, soft_value], axis=0)
    shards = {0: own}
    shards[4] = rotate(own, 4)
    shards[8] = rotate(own, 8)

    raw, state = linear_call(after(place, own), doc_lengths, lin_query, lin_key, lin_value)
    state_before = rotate(state, 4)
    for k in (1, 3, 2):
        shards[k] = behind(k, after(own, state), shards[4])
    sums = attend(after(place, state), None, True, (4,), False, "attend_a")

    pair = join_call(4, after(place, sums[1]), doc_lengths, state, state_before)
    pair_before = rotate(pair, 1)
    for k in (1, 3, 2):
        shards[k + 4] = behind(k, after(shards[4], pair), shards[8])
    sums = attend(after(place, pair), sums, False, (8, 1), False, "attend_b")

    four = join_call(1, after(place, sums[1]), doc_lengths, pair, pair_before)
    near, far = rotate(four, 1), rotate(four, 3)
    sums = attend(after(place, four), sums, False, (3, 2), False, "attend_c")

    raw, square = inter_call(after(place, sums[1]), doc_lengths, lin_query, near, far, raw)
    for bit in (1, 2):
        square = square + head_swap(square, bit)
    soft_out = attend(after(place, square), sums, False, (5, 7, 6), True, "attend_d")
    lin_out = norm_call(raw, lin_gate, gain, square, head_swap(square, 4))
    return lin_out, soft_out


def solution(mesh):
    split = P("ctx", "head")
    return jax.shard_map(
        body,
        mesh=mesh,
        in_specs=(split, split, split, split, P("head"), split, split, split, P()),
        out_specs=(split, split),
        check_vma=False,
    )
```

profile of v0, /device:TPU:6, one launch (start us, length us, event | category | flops | bytes accessed | tf_op | source)
XLA Modules:
  0.0 201.3 jit_solution(10649278085706353495)
XLA Ops:
  0.6 0.9 constant_dynamic-update-slice_fusion.1
  1.5 0.9 constant_dynamic-update-slice_fusion.refs_3_.refs_6_
  2.5 0.5 collective-permute-start
  2.9 0.0 copy-start.3
  2.9 0.0 copy-start.5
  2.9 5.7 %linear.1 = (f32[512,1024]{1,0:T(8,128)}, bf16[1024,128]{1,0:T(8,128)(2,1)}) custom-call(s32[1]{0:T(128)} %bitcast.place.refs_0_, s32[8]{0:T(128)} %refs_1_.7, bf16[512,1024]{1,0:T(8,128)(2,1)} %q_ref.3, bf16[512,1024]{1,0:T(8,128)(2,1)} %k_ref.1, bf16[512,1024]{1,0:T(8,128)(2,1)} %v_ref.1), custom_call_target="tpu_custom_call" | custom-call | flops 1000000 | bytes 65536 | tf_op jit(solution)/shard_map/linear/pallas_call | solution.py:95
  8.6 0.0 copy-start.4
  8.6 1.6 collective-permute-start.1
  10.2 2.1 %collective-permute-start.2 = (bf16[1024,128]{1,0:T(8,128)(2,1)S(1)}, bf16[1024,128]{1,0:T(8,128)(2,1)S(1)}, u32[]{:S(2)}, u32[]{:S(2)}) collective-permute-start(bf16[1024,128]{1,0:T(8,128)(2,1)S(1)} %constant_dynamic-update-slice_fusion.refs_3_.refs_6_), channel_id=1, source_target_pairs={{0,64},{8,72},{16,80},{24,88},{32,96},{40,104},{48,112},{56,120},{... | collective-permute-start | bytes 786440 | tf_op jit(solution)/shard_map/ppermute | solution.py:402
  12.3 0.0 collective-permute-done.refs_4_.refs_10_
  12.3 0.1 broadcast_select_fusion.1
  12.4 1.6 collective-permute-start.3
  14.0 0.0 copy-done.3
  14.0 0.0 copy-done.5
  14.0 5.7 %attend_a.1 = (f32[512,1024]{1,0:T(8,128)S(1)}, f32[512,1024]{1,0:T(8,128)S(1)}, bf16[512,1024]{1,0:T(8,128)(2,1)S(1)}) custom-call(s32[1]{0:T(128)} %bitcast.place.refs_0_, s32[8]{0:T(128)S(1)} %copy-done.5, bf16[512,1024]{1,0:T(8,128)(2,1)S(1)} %copy-done.3, bf16[1024,128]{1,0:T(8,128)(2,1)S(1)} %constant_dynamic-update-slice_fusion.refs_3_.refs_6_, ...), custom_call_target="tpu_custom_call" | custom-call | flops 1000000 | bytes 65536 | tf_op jit(solution)/shard_map/attend_a/pallas_call | solution.py:385
  19.8 0.0 collective-permute-done.1.got_ref
  19.8 0.0 copy-done.4
  19.8 0.6 join4.1.own_ref
  20.4 0.1 collective-permute-start.4
  20.5 2.8 %collective-permute-start.6 = (bf16[1024,128]{1,0:T(8,128)(2,1)S(1)}, bf16[1024,128]{1,0:T(8,128)(2,1)S(1)}, u32[]{:S(2)}, u32[]{:S(2)}) collective-permute-start(bf16[1024,128]{1,0:T(8,128)(2,1)S(1)} %get-tuple-element.47), channel_id=1, source_target_pairs={{0,16},{8,24},{16,0},{24,8},{32,48},{40,56},{48,32},{56,40},{64,80... | collective-permute-start | bytes 786440 | tf_op jit(solution)/shard_map/ppermute | solution.py:406
  23.3 5.0 %collective-permute-start.5 = (bf16[1024,128]{1,0:T(8,128)(2,1)S(1)}, bf16[1024,128]{1,0:T(8,128)(2,1)S(1)}, u32[]{:S(2)}, u32[]{:S(2)}) collective-permute-start(bf16[1024,128]{1,0:T(8,128)(2,1)S(1)} %get-tuple-element.48), channel_id=1, source_target_pairs={{0,24},{8,0},{16,8},{24,16},{32,56},{40,32},{48,40},{56,48},{64,88... | collective-permute-start | bytes 786440 | tf_op jit(solution)/shard_map/ppermute | solution.py:406
  28.4 0.0 collective-permute-done.2.refs_3_.refs_14_
  28.4 0.0 collective-permute-done.3.refs_4_.refs_7_
  28.4 6.0 %attend_b.1 = (f32[512,1024]{1,0:T(8,128)S(1)}, f32[512,1024]{1,0:T(8,128)S(1)}) custom-call(s32[1]{0:T(128)} %bitcast.place.refs_0_, s32[8]{0:T(128)S(1)} %copy-done.5, bf16[512,1024]{1,0:T(8,128)(2,1)S(1)} %get-tuple-element.29.refs_2_, ...), custom_call_target="tpu_custom_call", output_to_operand_aliasing={{0}: (5, {}), {1}: (6, {})} | custom-call | flops 1000000 | bytes 65536 | tf_op jit(solution)/shard_map/attend_b/pallas_call | solution.py:385
  34.4 0.0 collective-permute-done.4.got_ref
  34.4 0.6 join1.1
  35.1 0.1 collective-permute-start.8
  35.2 4.7 %collective-permute-start.7 = (bf16[1024,128]{1,0:T(8,128)(2,1)S(1)}, bf16[1024,128]{1,0:T(8,128)(2,1)S(1)}, u32[]{:S(2)}, u32[]{:S(2)}) collective-permute-start(bf16[1024,128]{1,0:T(8,128)(2,1)S(1)} %join1.1), channel_id=1, source_target_pairs={{0,8},{8,16},{16,24},{24,32},{32,40},{40,48},{48,56},{56,64},{64,7... | collective-permute-start | bytes 786440 | tf_op jit(solution)/shard_map/ppermute | solution.py:402
  39.9 0.1 broadcast_select_fusion
  39.9 0.1 collective-permute-start.14
  40.0 0.0 collective-permute-done.6.refs_4_.refs_8_
  40.1 2.7 %collective-permute-start.13 = (bf16[1024,128]{1,0:T(8,128)(2,1)S(1)}, bf16[1024,128]{1,0:T(8,128)(2,1)S(1)}, u32[]{:S(2)}, u32[]{:S(2)}) collective-permute-start(bf16[1024,128]{1,0:T(8,128)(2,1)S(1)} %get-tuple-element.45), channel_id=1, source_target_pairs={{0,24},{8,0},{16,8},{24,16},{32,56},{40,32},{48,40},{56,48},{64,88... | collective-permute-start | bytes 786440 | tf_op jit(solution)/shard_map/ppermute | solution.py:406
  42.7 0.2 collective-permute-done.5.refs_3_.refs_9_
  42.9 0.9 collective-permute-start.12
  43.7 0.0 copy-start
  43.7 0.0 copy-start.1
  43.7 5.8 %attend_c.1 = (f32[512,1024]{1,0:T(8,128)S(1)}, f32[512,1024]{1,0:T(8,128)S(1)}) custom-call(s32[1]{0:T(128)} %bitcast.place.refs_0_, s32[8]{0:T(128)S(1)} %copy-done.5, bf16[512,1024]{1,0:T(8,128)(2,1)S(1)} %get-tuple-element.29.refs_2_, bf16[1024,128]{1,0:T(8,128)(2,1)S(1)} %collective-permute-done.5.refs_3_.refs_9_, ...), custom_call_target="tpu_custom_call", output_to_operand_aliasing={{0}: (5, {}), {1}: (6, {})} | custom-call | flops 1000000 | bytes 65536 | tf_op jit(solution)/shard_map/attend_c/pallas_call | solution.py:385
  49.6 0.0 collective-permute-done.8.far_ref
  49.6 0.0 collective-permute-done.7.near_ref
  49.6 0.0 copy-done
  49.6 0.0 copy-done.1
  49.6 1.9 inter.1
  51.6 0.0 collective-permute-start.9
  51.6 1.2 collective-permute-done.9
  52.8 0.0 collective-permute-start.10
  52.8 3.7 %collective-permute-done.10 = f32[8,512]{1,0:T(8,128)S(1)} collective-permute-done((f32[8,512]{1,0:T(8,128)S(1)}, f32[8,512]{1,0:T(8,128)S(1)}, u32[]{:S(2)}, u32[]{:S(2)}) %collective-permute-start.10) | collective-permute-done | bytes 16416 | tf_op jit(solution)/shard_map/ppermute | solution.py:412
  56.5 1.9 collective-permute-start.11
  58.4 0.0 collective-permute-done.14.refs_5_.refs_12_
  58.4 0.0 collective-permute-done.13.refs_4_.refs_13_
  58.4 0.0 collective-permute-done.12.refs_3_.refs_11_
  58.4 0.0 copy-start.2
  58.4 0.0 copy-start.6
  58.4 140.9 %attend_d.1 = bf16[512,1024]{1,0:T(8,128)(2,1)} custom-call(s32[1]{0:T(128)} %bitcast.place.refs_0_, s32[8]{0:T(128)S(1)} %copy-done.5, bf16[512,1024]{1,0:T(8,128)(2,1)S(1)} %get-tuple-element.29.refs_2_, bf16[1024,128]{1,0:T(8,128)(2,1)S(1)} %collective-permute-done.12.refs_3_.refs_11_, bf16[1024,128]{1,0:T(8,128)(2,1)S(1)} %collective-permute-done.13.refs_4_.refs_13_, ...), custom_call_target="tpu_custom_call" | custom-call | flops 1000000 | bytes 65536 | tf_op jit(solution)/shard_map/attend_d/pallas_call | solution.py:385
  199.3 0.0 collective-permute-done.11.far_ref
  199.3 0.0 copy-done.2
  199.3 0.0 copy-done.6
  199.3 2.0 norm.1
  (2 shorter events, 0.0 us)
Async XLA Ops:
  2.5 9.9 %collective-permute-start = (bf16[1024,128]{1,0:T(8,128)(2,1)S(1)}, bf16[1024,128]{1,0:T(8,128)(2,1)S(1)}, u32[]{:S(2)}, u32[]{:S(2)}) collective-permute-start(bf16[1024,128]{1,0:T(8,128)(2,1)S(1)} %constant_dynamic-update-slice_fusion.refs_3_.refs_6_), channel_id=1, source_target_pairs={{0,32},{8,40},{16,48},{24,56},{32,64},{40,72},{48,80},{56,88},{64,... | collective-permute-start | bytes 786440 | tf_op jit(solution)/shard_map/ppermute | solution.py:402
  2.9 11.1 %copy-start.3 = (bf16[512,1024]{1,0:T(8,128)(2,1)S(1)}, bf16[512,1024]{1,0:T(8,128)(2,1)}, u32[]{:S(2)}) copy-start(bf16[512,1024]{1,0:T(8,128)(2,1)} %refs_2_.1) | copy-start | bytes 3145732
  2.9 11.1 %copy-start.5 = (s32[8]{0:T(128)S(1)}, s32[8]{0:T(128)}, u32[]{:S(2)}) copy-start(s32[8]{0:T(128)} %refs_1_.7) | copy-start | bytes 100
  8.6 11.2 %copy-start.4 = (bf16[1024,128]{1,0:T(8,128)(2,1)S(1)}, bf16[1024,128]{1,0:T(8,128)(2,1)}, u32[]{:S(2)}) copy-start(bf16[1024,128]{1,0:T(8,128)(2,1)} %get-tuple-element.24.own_ref) | copy-start | bytes 786436
  8.6 11.1 %collective-permute-start.1 = (bf16[1024,128]{1,0:T(8,128)(2,1)}, bf16[1024,128]{1,0:T(8,128)(2,1)S(1)}, u32[]{:S(2)}, u32[]{:S(2)}) collective-permute-start(bf16[1024,128]{1,0:T(8,128)(2,1)} %get-tuple-element.24.own_ref), channel_id=1, source_target_pairs={{0,32},{8,40},{16,48},{24,56},{32,64},{40,72},{48,80},{56,88},{64,... | collective-permute-start | bytes 786440 | tf_op jit(solution)/shard_map/ppermute | solution.py:402
  10.2 18.2 %collective-permute-start.2 = (bf16[1024,128]{1,0:T(8,128)(2,1)S(1)}, bf16[1024,128]{1,0:T(8,128)(2,1)S(1)}, u32[]{:S(2)}, u32[]{:S(2)}) collective-permute-start(bf16[1024,128]{1,0:T(8,128)(2,1)S(1)} %constant_dynamic-update-slice_fusion.refs_3_.refs_6_), channel_id=1, source_target_pairs={{0,64},{8,72},{16,80},{24,88},{32,96},{40,104},{48,112},{56,120},{... | collective-permute-start | bytes 786440 | tf_op jit(solution)/shard_map/ppermute | solution.py:402
  12.4 16.0 %collective-permute-start.3 = (bf16[1024,128]{1,0:T(8,128)(2,1)S(1)}, bf16[1024,128]{1,0:T(8,128)(2,1)S(1)}, u32[]{:S(2)}, u32[]{:S(2)}) collective-permute-start(bf16[1024,128]{1,0:T(8,128)(2,1)S(1)} %get-tuple-element.49), channel_id=1, source_target_pairs={{0,8},{8,16},{16,24},{24,0},{32,40},{40,48},{48,56},{56,32},{64,72... | collective-permute-start | bytes 786440 | tf_op jit(solution)/shard_map/ppermute | solution.py:406
  20.4 14.0 %collective-permute-start.4 = (bf16[1024,128]{1,0:T(8,128)(2,1)S(1)}, bf16[1024,128]{1,0:T(8,128)(2,1)S(1)}, u32[]{:S(2)}, u32[]{:S(2)}) collective-permute-start(bf16[1024,128]{1,0:T(8,128)(2,1)S(1)} %join4.1.own_ref), channel_id=1, source_target_pairs={{0,8},{8,16},{16,24},{24,32},{32,40},{40,48},{48,56},{56,64},{64,7... | collective-permute-start | bytes 786440 | tf_op jit(solution)/shard_map/ppermute | solution.py:402
  20.5 19.5 %collective-permute-start.6 = (bf16[1024,128]{1,0:T(8,128)(2,1)S(1)}, bf16[1024,128]{1,0:T(8,128)(2,1)S(1)}, u32[]{:S(2)}, u32[]{:S(2)}) collective-permute-start(bf16[1024,128]{1,0:T(8,128)(2,1)S(1)} %get-tuple-element.47), channel_id=1, source_target_pairs={{0,16},{8,24},{16,0},{24,8},{32,48},{40,56},{48,32},{56,40},{64,80... | collective-permute-start | bytes 786440 | tf_op jit(solution)/shard_map/ppermute | solution.py:406
  23.3 19.5 %collective-permute-start.5 = (bf16[1024,128]{1,0:T(8,128)(2,1)S(1)}, bf16[1024,128]{1,0:T(8,128)(2,1)S(1)}, u32[]{:S(2)}, u32[]{:S(2)}) collective-permute-start(bf16[1024,128]{1,0:T(8,128)(2,1)S(1)} %get-tuple-element.48), channel_id=1, source_target_pairs={{0,24},{8,0},{16,8},{24,16},{32,56},{40,32},{48,40},{56,48},{64,88... | collective-permute-start | bytes 786440 | tf_op jit(solution)/shard_map/ppermute | solution.py:406
  35.1 14.5 %collective-permute-start.8 = (bf16[1024,128]{1,0:T(8,128)(2,1)S(1)}, bf16[1024,128]{1,0:T(8,128)(2,1)S(1)}, u32[]{:S(2)}, u32[]{:S(2)}) collective-permute-start(bf16[1024,128]{1,0:T(8,128)(2,1)S(1)} %join1.1), channel_id=1, source_target_pairs={{0,24},{8,32},{16,40},{24,48},{32,56},{40,64},{48,72},{56,80},{64,... | collective-permute-start | bytes 786440 | tf_op jit(solution)/shard_map/ppermute | solution.py:402
  35.2 14.4 %collective-permute-start.7 = (bf16[1024,128]{1,0:T(8,128)(2,1)S(1)}, bf16[1024,128]{1,0:T(8,128)(2,1)S(1)}, u32[]{:S(2)}, u32[]{:S(2)}) collective-permute-start(bf16[1024,128]{1,0:T(8,128)(2,1)S(1)} %join1.1), channel_id=1, source_target_pairs={{0,8},{8,16},{16,24},{24,32},{32,40},{40,48},{48,56},{56,64},{64,7... | collective-permute-start | bytes 786440 | tf_op jit(solution)/shard_map/ppermute | solution.py:402
  39.9 18.4 %collective-permute-start.14 = (bf16[1024,128]{1,0:T(8,128)(2,1)S(1)}, bf16[1024,128]{1,0:T(8,128)(2,1)S(1)}, u32[]{:S(2)}, u32[]{:S(2)}) collective-permute-start(bf16[1024,128]{1,0:T(8,128)(2,1)S(1)} %get-tuple-element.44), channel_id=1, source_target_pairs={{0,16},{8,24},{16,0},{24,8},{32,48},{40,56},{48,32},{56,40},{64,80... | collective-permute-start | bytes 786440 | tf_op jit(solution)/shard_map/ppermute | solution.py:406
  40.1 18.3 %collective-permute-start.13 = (bf16[1024,128]{1,0:T(8,128)(2,1)S(1)}, bf16[1024,128]{1,0:T(8,128)(2,1)S(1)}, u32[]{:S(2)}, u32[]{:S(2)}) collective-permute-start(bf16[1024,128]{1,0:T(8,128)(2,1)S(1)} %get-tuple-element.45), channel_id=1, source_target_pairs={{0,24},{8,0},{16,8},{24,16},{32,56},{40,32},{48,40},{56,48},{64,88... | collective-permute-start | bytes 786440 | tf_op jit(solution)/shard_map/ppermute | solution.py:406
  42.9 15.5 %collective-permute-start.12 = (bf16[1024,128]{1,0:T(8,128)(2,1)S(1)}, bf16[1024,128]{1,0:T(8,128)(2,1)S(1)}, u32[]{:S(2)}, u32[]{:S(2)}) collective-permute-start(bf16[1024,128]{1,0:T(8,128)(2,1)S(1)} %get-tuple-element.46), channel_id=1, source_target_pairs={{0,8},{8,16},{16,24},{24,0},{32,40},{40,48},{48,56},{56,32},{64,72... | collective-permute-start | bytes 786440 | tf_op jit(solution)/shard_map/ppermute | solution.py:406
  43.7 5.9 %copy-start = (f32[512,1024]{1,0:T(8,128)S(1)}, f32[512,1024]{1,0:T(8,128)}, u32[]{:S(2)}) copy-start(f32[512,1024]{1,0:T(8,128)} %get-tuple-element.38.raw_ref) | copy-start | bytes 6291460
  43.7 5.9 %copy-start.1 = (bf16[512,1024]{1,0:T(8,128)(2,1)S(1)}, bf16[512,1024]{1,0:T(8,128)(2,1)}, u32[]{:S(2)}) copy-start(bf16[512,1024]{1,0:T(8,128)(2,1)} %q_ref.3) | copy-start | bytes 3145732
  51.6 1.2 collective-permute-start.9
  52.8 3.7 %collective-permute-start.10 = (f32[8,512]{1,0:T(8,128)S(1)}, f32[8,512]{1,0:T(8,128)S(1)}, u32[]{:S(2)}, u32[]{:S(2)}) collective-permute-start(f32[8,512]{1,0:T(8,128)S(1)} %add.11), channel_id=1, source_target_pairs={{0,2},{1,3},{2,0},{3,1},{4,6},{5,7},{6,4},{7,5},{8,10},{9,11},{10,... | collective-permute-start | bytes 49160 | tf_op jit(solution)/shard_map/ppermute | solution.py:412
  56.5 142.8 %collective-permute-start.11 = (f32[8,512]{1,0:T(8,128)S(1)}, f32[8,512]{1,0:T(8,128)S(1)}, u32[]{:S(2)}, u32[]{:S(2)}) collective-permute-start(f32[8,512]{1,0:T(8,128)S(1)} %add.12.near_ref), channel_id=1, source_target_pairs={{0,4},{1,5},{2,6},{3,7},{4,0},{5,1},{6,2},{7,3},{8,12},{9,13},{10,... | collective-permute-start | bytes 49160 | tf_op jit(solution)/shard_map/ppermute | solution.py:412
  58.4 140.9 %copy-start.2 = (bf16[512,1024]{1,0:T(8,128)(2,1)S(1)}, bf16[512,1024]{1,0:T(8,128)(2,1)}, u32[]{:S(2)}) copy-start(bf16[512,1024]{1,0:T(8,128)(2,1)} %gate_ref.1) | copy-start | bytes 3145732
  58.4 140.9 %copy-start.6 = (f32[1024]{0:T(1024)S(1)}, f32[1024]{0:T(1024)}, u32[]{:S(2)}) copy-start(f32[1024]{0:T(1024)} %param.13) | copy-start | bytes 12292
where the time goes:
time: 202 us; the launch traced here: 201 us
  Pallas kernels  169 us (84%)
  starting transfers between devices  24 us (12%)
  waiting for transfers between devices  5.13 us (3%)
    pallas_call x4, Pallas kernels, attend_call(): pl.pallas_call(functools.partial(attend_kernel, tuple(offsets), own, firs...  158 us
    ppermute x6, starting transfers between devices, turn(): lax.ppermute(a, 'ctx', [(4 * x + y, 4 * x + (y + distance) % 4) for x in...  13.1 us
    ppermute x6, starting transfers between devices, rotate(): return lax.ppermute(a, 'ctx', [(c, (c + distance) % 16) for c in range(16)])  9.04 us
    pallas_call x1, Pallas kernels, linear_call(): pl.pallas_call(linear_kernel, grid=(LOCAL * HEAD_DIM // step,), in_specs=...  5.68 us
    ppermute x3, waiting for transfers between devices, head_swap(): return lax.ppermute(a, 'head', [(i, i ^ bit) for i in range(8)])  4.95 us
  transfers between devices with their start and end apart: 15, of which 3 were waited for; matrix products, arithmetic and copies ran while one was open for 0% of the time, Pallas kernels for 83%

commit v1 on v0

--- a/solution.py
+++ b/solution.py
@@ -442,13 +442,14 @@
 
     pair = join_call(4, after(place, sums[1]), doc_lengths, state, state_before)
     pair_before = rotate(pair, 1)
-    for k in (1, 3, 2):
+    for k in (1, 3):
         shards[k + 4] = behind(k, after(shards[4], pair), shards[8])
-    sums = attend(after(place, pair), sums, False, (8, 1), False, "attend_b")
+    shards[6] = rotate(after(shards[2], pair), 4)
+    sums = attend(after(place, pair), sums, False, (8, 1, 3), False, "attend_b")
 
     four = join_call(1, after(place, sums[1]), doc_lengths, pair, pair_before)
     near, far = rotate(four, 1), rotate(four, 3)
-    sums = attend(after(place, four), sums, False, (3, 2), False, "attend_c")
+    sums = attend(after(place, four), sums, False, (2,), False, "attend_c")
 
     raw, square = inter_call(after(place, sums[1]), doc_lengths, lin_query, near, far, raw)
     for bit in (1, 2):

time: 202 us -> 202 us (level)
  the two profiles are of different devices: /device:TPU:6 before, /device:TPU:4 now
where the time goes in v1:
time: 202 us
  Pallas kernels  164 us (81%)
  starting transfers between devices  22.3 us (11%)
  waiting for transfers between devices  13 us (6%)
    pallas_call x4, Pallas kernels, attend_call(): pl.pallas_call(functools.partial(attend_kernel, tuple(offsets), own, firs...  153 us
    ppermute x7, waiting for transfers between devices, rotate(): return lax.ppermute(a, 'ctx', [(c, (c + distance) % 16) for c in range(16)])  9.95 us
    ppermute x7, starting transfers between devices, rotate(): return lax.ppermute(a, 'ctx', [(c, (c + distance) % 16) for c in range(16)])  9.45 us
    ppermute x5, starting transfers between devices, turn(): lax.ppermute(a, 'ctx', [(4 * x + y, 4 * x + (y + distance) % 4) for x in...  7.07 us
    ppermute x3, starting transfers between devices, head_swap(): return lax.ppermute(a, 'head', [(i, i ^ bit) for i in range(8)])  5.81 us
    pallas_call x1, Pallas kernels, linear_call(): pl.pallas_call(linear_kernel, grid=(LOCAL * HEAD_DIM // step,), in_specs=...  5.68 us
  transfers between devices with their start and end apart: 15, of which 4 were waited for; matrix products, arithmetic and copies ran while one was open for 0% of the time, Pallas kernels for 80%

profile of v1, /device:TPU:4, one launch (start us, length us, event | category | flops | bytes accessed | tf_op | source)
XLA Modules:
  0.0 201.6 jit_solution(17033679915484922670)
XLA Ops:
  0.6 0.9 constant_dynamic-update-slice_fusion.1
  1.5 0.9 constant_dynamic-update-slice_fusion.refs_3_.refs_6_
  2.5 1.3 collective-permute-start
  3.7 0.0 copy-start.3
  3.7 0.0 copy-start.5
  3.7 5.7 %linear.1 = (f32[512,1024]{1,0:T(8,128)}, bf16[1024,128]{1,0:T(8,128)(2,1)}) custom-call(s32[1]{0:T(128)} %bitcast.place.refs_0_, s32[8]{0:T(128)} %refs_1_.7, bf16[512,1024]{1,0:T(8,128)(2,1)} %q_ref.3, bf16[512,1024]{1,0:T(8,128)(2,1)} %k_ref.1, bf16[512,1024]{1,0:T(8,128)(2,1)} %v_ref.1), custom_call_target="tpu_custom_call" | custom-call | flops 1000000 | bytes 65536 | tf_op jit(solution)/shard_map/linear/pallas_call | solution.py:95
  9.4 0.0 copy-start.4
  9.4 0.4 collective-permute-start.1
  9.8 1.9 collective-permute-start.2
  11.7 0.0 collective-permute-done.refs_4_.refs_10_
  11.7 0.1 broadcast_select_fusion
  11.8 3.1 %collective-permute-start.4 = (bf16[1024,128]{1,0:T(8,128)(2,1)S(1)}, bf16[1024,128]{1,0:T(8,128)(2,1)S(1)}, u32[]{:S(2)}, u32[]{:S(2)}) collective-permute-start(bf16[1024,128]{1,0:T(8,128)(2,1)S(1)} %get-tuple-element.49), channel_id=1, source_target_pairs={{0,24},{8,0},{16,8},{24,16},{32,56},{40,32},{48,40},{56,48},{64,88... | collective-permute-start | bytes 786440 | tf_op jit(solution)/shard_map/ppermute | solution.py:406
  14.9 0.0 collective-permute-start.3
  14.9 0.0 copy-done.3
  14.9 0.0 copy-done.5
  14.9 5.7 %attend_a.1 = (f32[512,1024]{1,0:T(8,128)S(1)}, f32[512,1024]{1,0:T(8,128)S(1)}, bf16[512,1024]{1,0:T(8,128)(2,1)S(1)}) custom-call(s32[1]{0:T(128)} %bitcast.place.refs_0_, s32[8]{0:T(128)S(1)} %copy-done.5, bf16[512,1024]{1,0:T(8,128)(2,1)S(1)} %copy-done.3, bf16[1024,128]{1,0:T(8,128)(2,1)S(1)} %constant_dynamic-update-slice_fusion.refs_3_.refs_6_, ...), custom_call_target="tpu_custom_call" | custom-call | flops 1000000 | bytes 65536 | tf_op jit(solution)/shard_map/attend_a/pallas_call | solution.py:385
  20.6 0.0 collective-permute-done.1.got_ref
  20.6 0.0 copy-done.4
  20.6 0.6 join4.1.own_ref
  21.3 0.7 collective-permute-start.5
  21.9 1.9 collective-permute-start.6
  23.8 0.0 collective-permute-done.2.refs_3_.refs_14_
  23.8 0.0 collective-permute-done.4.refs_5_.refs_9_
  23.8 0.0 collective-permute-done.3.refs_4_.refs_7_
  23.8 5.8 %attend_b.1 = (f32[512,1024]{1,0:T(8,128)S(1)}, f32[512,1024]{1,0:T(8,128)S(1)}) custom-call(s32[1]{0:T(128)} %bitcast.place.refs_0_, s32[8]{0:T(128)S(1)} %copy-done.5, bf16[512,1024]{1,0:T(8,128)(2,1)S(1)} %get-tuple-element.30.refs_2_, ...), custom_call_target="tpu_custom_call", output_to_operand_aliasing={{0}: (6, {}), {1}: (7, {})} | custom-call | flops 1000000 | bytes 65536 | tf_op jit(solution)/shard_map/attend_b/pallas_call | solution.py:385
  29.6 5.6 %collective-permute-done.5.got_ref = bf16[1024,128]{1,0:T(8,128)(2,1)S(1)} collective-permute-done((bf16[1024,128]{1,0:T(8,128)(2,1)S(1)}, bf16[1024,128]{1,0:T(8,128)(2,1)S(1)}, u32[]{:S(2)}, u32[]{:S(2)}) %collective-permute-start.5) | collective-permute-done | bytes 262176 | tf_op jit(solution)/shard_map/ppermute | solution.py:402
  35.2 0.6 join1.1
  35.8 0.1 collective-permute-start.8
  35.9 1.1 collective-permute-start.7
  37.1 1.4 collective-permute-start.13
  38.4 0.7 collective-permute-start.12
  39.2 0.0 collective-permute-done.6.refs_3_.refs_8_
  39.2 4.0 %collective-permute-start.14 = (bf16[1024,128]{1,0:T(8,128)(2,1)S(1)}, bf16[1024,128]{1,0:T(8,128)(2,1)S(1)}, u32[]{:S(2)}, u32[]{:S(2)}) collective-permute-start(bf16[1024,128]{1,0:T(8,128)(2,1)S(1)} %collective-permute-done.6.refs_3_.refs_8_), channel_id=1, source_target_pairs={{0,32},{8,40},{16,48},{24,56},{32,64},{40,72},{48,80},{56,88},{64,... | collective-permute-start | bytes 786440 | tf_op jit(solution)/shard_map/ppermute | solution.py:402
  43.2 0.0 copy-start
  43.2 0.0 copy-start.1
  43.2 3.1 %attend_c.1 = (f32[512,1024]{1,0:T(8,128)S(1)}, f32[512,1024]{1,0:T(8,128)S(1)}) custom-call(s32[1]{0:T(128)} %bitcast.place.refs_0_, s32[8]{0:T(128)S(1)} %copy-done.5, bf16[512,1024]{1,0:T(8,128)(2,1)S(1)} %get-tuple-element.30.refs_2_, bf16[1024,128]{1,0:T(8,128)(2,1)S(1)} %collective-permute-done.6.refs_3_.refs_8_, ...), custom_call_target="tpu_custom_call", output_to_operand_aliasing={{0}: (4, {}), {1}: (5, {})} | custom-call | flops 1000000 | bytes 65536 | tf_op jit(solution)/shard_map/attend_c/pallas_call | solution.py:385
  46.3 0.0 collective-permute-done.8.far_ref
  46.3 4.4 %collective-permute-done.7.near_ref = bf16[1024,128]{1,0:T(8,128)(2,1)S(1)} collective-permute-done((bf16[1024,128]{1,0:T(8,128)(2,1)S(1)}, bf16[1024,128]{1,0:T(8,128)(2,1)S(1)}, u32[]{:S(2)}, u32[]{:S(2)}) %collective-permute-start.7) | collective-permute-done | bytes 262176 | tf_op jit(solution)/shard_map/ppermute | solution.py:402
  50.6 0.0 copy-done
  50.6 0.0 copy-done.1
  50.6 1.9 inter.1
  52.6 0.0 collective-permute-start.9
  52.6 1.2 collective-permute-done.9
  53.8 1.9 collective-permute-start.10
  55.7 1.8 collective-permute-done.10
  57.5 3.9 %collective-permute-start.11 = (f32[8,512]{1,0:T(8,128)S(1)}, f32[8,512]{1,0:T(8,128)S(1)}, u32[]{:S(2)}, u32[]{:S(2)}) collective-permute-start(f32[8,512]{1,0:T(8,128)S(1)} %add.12.near_ref), channel_id=1, source_target_pairs={{0,4},{1,5},{2,6},{3,7},{4,0},{5,1},{6,2},{7,3},{8,12},{9,13},{10,... | collective-permute-start | bytes 49160 | tf_op jit(solution)/shard_map/ppermute | solution.py:412
  61.4 0.0 collective-permute-done.13.refs_4_.refs_13_
  61.4 0.0 collective-permute-done.12.refs_3_.refs_11_
  61.4 0.0 collective-permute-done.14.refs_5_.refs_12_
  61.4 0.0 copy-start.2
  61.5 0.0 copy-start.6
  61.5 138.1 %attend_d.1 = bf16[512,1024]{1,0:T(8,128)(2,1)} custom-call(s32[1]{0:T(128)} %bitcast.place.refs_0_, s32[8]{0:T(128)S(1)} %copy-done.5, bf16[512,1024]{1,0:T(8,128)(2,1)S(1)} %get-tuple-element.30.refs_2_, bf16[1024,128]{1,0:T(8,128)(2,1)S(1)} %collective-permute-done.12.refs_3_.refs_11_, bf16[1024,128]{1,0:T(8,128)(2,1)S(1)} %collective-permute-done.13.refs_4_.refs_13_, ...), custom_call_target="tpu_custom_call" | custom-call | flops 1000000 | bytes 65536 | tf_op jit(solution)/shard_map/attend_d/pallas_call | solution.py:385
  199.6 0.0 collective-permute-done.11.far_ref
  199.6 0.0 copy-done.2
  199.6 0.0 copy-done.6
  199.6 2.0 norm.1
  (3 shorter events, 0.0 us)
Async XLA Ops:
  2.5 9.2 %collective-permute-start = (bf16[1024,128]{1,0:T(8,128)(2,1)S(1)}, bf16[1024,128]{1,0:T(8,128)(2,1)S(1)}, u32[]{:S(2)}, u32[]{:S(2)}) collective-permute-start(bf16[1024,128]{1,0:T(8,128)(2,1)S(1)} %constant_dynamic-update-slice_fusion.refs_3_.refs_6_), channel_id=1, source_target_pairs={{0,32},{8,40},{16,48},{24,56},{32,64},{40,72},{48,80},{56,88},{64,... | collective-permute-start | bytes 786440 | tf_op jit(solution)/shard_map/ppermute | solution.py:402
  3.7 11.1 %copy-start.3 = (bf16[512,1024]{1,0:T(8,128)(2,1)S(1)}, bf16[512,1024]{1,0:T(8,128)(2,1)}, u32[]{:S(2)}) copy-start(bf16[512,1024]{1,0:T(8,128)(2,1)} %refs_2_.1) | copy-start | bytes 3145732
  3.7 11.1 %copy-start.5 = (s32[8]{0:T(128)S(1)}, s32[8]{0:T(128)}, u32[]{:S(2)}) copy-start(s32[8]{0:T(128)} %refs_1_.7) | copy-start | bytes 100
  9.4 11.2 %copy-start.4 = (bf16[1024,128]{1,0:T(8,128)(2,1)S(1)}, bf16[1024,128]{1,0:T(8,128)(2,1)}, u32[]{:S(2)}) copy-start(bf16[1024,128]{1,0:T(8,128)(2,1)} %get-tuple-element.25.own_ref) | copy-start | bytes 786436
  9.4 11.2 %collective-permute-start.1 = (bf16[1024,128]{1,0:T(8,128)(2,1)}, bf16[1024,128]{1,0:T(8,128)(2,1)S(1)}, u32[]{:S(2)}, u32[]{:S(2)}) collective-permute-start(bf16[1024,128]{1,0:T(8,128)(2,1)} %get-tuple-element.25.own_ref), channel_id=1, source_target_pairs={{0,32},{8,40},{16,48},{24,56},{32,64},{40,72},{48,80},{56,88},{64,... | collective-permute-start | bytes 786440 | tf_op jit(solution)/shard_map/ppermute | solution.py:402
  9.8 14.0 %collective-permute-start.2 = (bf16[1024,128]{1,0:T(8,128)(2,1)S(1)}, bf16[1024,128]{1,0:T(8,128)(2,1)S(1)}, u32[]{:S(2)}, u32[]{:S(2)}) collective-permute-start(bf16[1024,128]{1,0:T(8,128)(2,1)S(1)} %constant_dynamic-update-slice_fusion.refs_3_.refs_6_), channel_id=1, source_target_pairs={{0,64},{8,72},{16,80},{24,88},{32,96},{40,104},{48,112},{56,120},{... | collective-permute-start | bytes 786440 | tf_op jit(solution)/shard_map/ppermute | solution.py:402
  11.8 12.0 %collective-permute-start.4 = (bf16[1024,128]{1,0:T(8,128)(2,1)S(1)}, bf16[1024,128]{1,0:T(8,128)(2,1)S(1)}, u32[]{:S(2)}, u32[]{:S(2)}) collective-permute-start(bf16[1024,128]{1,0:T(8,128)(2,1)S(1)} %get-tuple-element.49), channel_id=1, source_target_pairs={{0,24},{8,0},{16,8},{24,16},{32,56},{40,32},{48,40},{56,48},{64,88... | collective-permute-start | bytes 786440 | tf_op jit(solution)/shard_map/ppermute | solution.py:406
  14.9 8.9 %collective-permute-start.3 = (bf16[1024,128]{1,0:T(8,128)(2,1)S(1)}, bf16[1024,128]{1,0:T(8,128)(2,1)S(1)}, u32[]{:S(2)}, u32[]{:S(2)}) collective-permute-start(bf16[1024,128]{1,0:T(8,128)(2,1)S(1)} %get-tuple-element.50), channel_id=1, source_target_pairs={{0,8},{8,16},{16,24},{24,0},{32,40},{40,48},{48,56},{56,32},{64,72... | collective-permute-start | bytes 786440 | tf_op jit(solution)/shard_map/ppermute | solution.py:406
  21.3 13.9 %collective-permute-start.5 = (bf16[1024,128]{1,0:T(8,128)(2,1)S(1)}, bf16[1024,128]{1,0:T(8,128)(2,1)S(1)}, u32[]{:S(2)}, u32[]{:S(2)}) collective-permute-start(bf16[1024,128]{1,0:T(8,128)(2,1)S(1)} %join4.1.own_ref), channel_id=1, source_target_pairs={{0,8},{8,16},{16,24},{24,32},{32,40},{40,48},{48,56},{56,64},{64,7... | collective-permute-start | bytes 786440 | tf_op jit(solution)/shard_map/ppermute | solution.py:402
  21.9 17.3 %collective-permute-start.6 = (bf16[1024,128]{1,0:T(8,128)(2,1)S(1)}, bf16[1024,128]{1,0:T(8,128)(2,1)S(1)}, u32[]{:S(2)}, u32[]{:S(2)}) collective-permute-start(bf16[1024,128]{1,0:T(8,128)(2,1)S(1)} %get-tuple-element.48), channel_id=1, source_target_pairs={{0,16},{8,24},{16,0},{24,8},{32,48},{40,56},{48,32},{56,40},{64,80... | collective-permute-start | bytes 786440 | tf_op jit(solution)/shard_map/ppermute | solution.py:406
  35.8 10.5 %collective-permute-start.8 = (bf16[1024,128]{1,0:T(8,128)(2,1)S(1)}, bf16[1024,128]{1,0:T(8,128)(2,1)S(1)}, u32[]{:S(2)}, u32[]{:S(2)}) collective-permute-start(bf16[1024,128]{1,0:T(8,128)(2,1)S(1)} %join1.1), channel_id=1, source_target_pairs={{0,24},{8,32},{16,40},{24,48},{32,56},{40,64},{48,72},{56,80},{64,... | collective-permute-start | bytes 786440 | tf_op jit(solution)/shard_map/ppermute | solution.py:402
  35.9 14.8 %collective-permute-start.7 = (bf16[1024,128]{1,0:T(8,128)(2,1)S(1)}, bf16[1024,128]{1,0:T(8,128)(2,1)S(1)}, u32[]{:S(2)}, u32[]{:S(2)}) collective-permute-start(bf16[1024,128]{1,0:T(8,128)(2,1)S(1)} %join1.1), channel_id=1, source_target_pairs={{0,8},{8,16},{16,24},{24,32},{32,40},{40,48},{48,56},{56,64},{64,7... | collective-permute-start | bytes 786440 | tf_op jit(solution)/shard_map/ppermute | solution.py:402
  37.1 24.4 %collective-permute-start.13 = (bf16[1024,128]{1,0:T(8,128)(2,1)S(1)}, bf16[1024,128]{1,0:T(8,128)(2,1)S(1)}, u32[]{:S(2)}, u32[]{:S(2)}) collective-permute-start(bf16[1024,128]{1,0:T(8,128)(2,1)S(1)} %get-tuple-element.46), channel_id=1, source_target_pairs={{0,24},{8,0},{16,8},{24,16},{32,56},{40,32},{48,40},{56,48},{64,88... | collective-permute-start | bytes 786440 | tf_op jit(solution)/shard_map/ppermute | solution.py:406
  38.4 23.0 %collective-permute-start.12 = (bf16[1024,128]{1,0:T(8,128)(2,1)S(1)}, bf16[1024,128]{1,0:T(8,128)(2,1)S(1)}, u32[]{:S(2)}, u32[]{:S(2)}) collective-permute-start(bf16[1024,128]{1,0:T(8,128)(2,1)S(1)} %get-tuple-element.47), channel_id=1, source_target_pairs={{0,8},{8,16},{16,24},{24,0},{32,40},{40,48},{48,56},{56,32},{64,72... | collective-permute-start | bytes 786440 | tf_op jit(solution)/shard_map/ppermute | solution.py:406
  39.2 22.3 %collective-permute-start.14 = (bf16[1024,128]{1,0:T(8,128)(2,1)S(1)}, bf16[1024,128]{1,0:T(8,128)(2,1)S(1)}, u32[]{:S(2)}, u32[]{:S(2)}) collective-permute-start(bf16[1024,128]{1,0:T(8,128)(2,1)S(1)} %collective-permute-done.6.refs_3_.refs_8_), channel_id=1, source_target_pairs={{0,32},{8,40},{16,48},{24,56},{32,64},{40,72},{48,80},{56,88},{64,... | collective-permute-start | bytes 786440 | tf_op jit(solution)/shard_map/ppermute | solution.py:402
  43.2 7.5 %copy-start = (f32[512,1024]{1,0:T(8,128)S(1)}, f32[512,1024]{1,0:T(8,128)}, u32[]{:S(2)}) copy-start(f32[512,1024]{1,0:T(8,128)} %get-tuple-element.39.raw_ref) | copy-start | bytes 6291460
  43.2 7.5 %copy-start.1 = (bf16[512,1024]{1,0:T(8,128)(2,1)S(1)}, bf16[512,1024]{1,0:T(8,128)(2,1)}, u32[]{:S(2)}) copy-start(bf16[512,1024]{1,0:T(8,128)(2,1)} %q_ref.3) | copy-start | bytes 3145732
  52.6 1.2 collective-permute-start.9
  53.8 3.7 %collective-permute-start.10 = (f32[8,512]{1,0:T(8,128)S(1)}, f32[8,512]{1,0:T(8,128)S(1)}, u32[]{:S(2)}, u32[]{:S(2)}) collective-permute-start(f32[8,512]{1,0:T(8,128)S(1)} %add.11), channel_id=1, source_target_pairs={{0,2},{1,3},{2,0},{3,1},{4,6},{5,7},{6,4},{7,5},{8,10},{9,11},{10,... | collective-permute-start | bytes 49160 | tf_op jit(solution)/shard_map/ppermute | solution.py:412
  57.5 142.0 %collective-permute-start.11 = (f32[8,512]{1,0:T(8,128)S(1)}, f32[8,512]{1,0:T(8,128)S(1)}, u32[]{:S(2)}, u32[]{:S(2)}) collective-permute-start(f32[8,512]{1,0:T(8,128)S(1)} %add.12.near_ref), channel_id=1, source_target_pairs={{0,4},{1,5},{2,6},{3,7},{4,0},{5,1},{6,2},{7,3},{8,12},{9,13},{10,... | collective-permute-start | bytes 49160 | tf_op jit(solution)/shard_map/ppermute | solution.py:412
  61.4 138.2 %copy-start.2 = (bf16[512,1024]{1,0:T(8,128)(2,1)S(1)}, bf16[512,1024]{1,0:T(8,128)(2,1)}, u32[]{:S(2)}) copy-start(bf16[512,1024]{1,0:T(8,128)(2,1)} %gate_ref.1) | copy-start | bytes 3145732
  61.5 138.2 %copy-start.6 = (f32[1024]{0:T(1024)S(1)}, f32[1024]{0:T(1024)}, u32[]{:S(2)}) copy-start(f32[1024]{0:T(1024)} %param.13) | copy-start | bytes 12292
